TPU v7x, 32 devices: a whole 2x2x4 slice. The times are simulated.
32 devices in a mesh: kv: 2 (over y), ex: 16 (over z, x, core).
Axes of the slice: x: 2, y: 2, z: 4, core: 2. Of those that a mesh axis runs over, the one named last changes fastest.
Arguments:
- x_tokens: bfloat16 [16, 576, 2048], P('ex'), may hold values from -6 to 6
- attn_gain: float32 [2048], replicated, may hold values from 0.1 to 1.9
- w_qkv: bfloat16 [2048, 3, 2048], P(None, None, 'kv'), may hold values from -1 to 1
- w_out: bfloat16 [2048, 2048], P('kv'), may hold values from -0.125 to 0.125
- cache: bfloat16 [32, 2, 512, 2048], P('ex', None, None, 'kv'), may hold values from -6 to 6
- cache_len: int32 [32], P('ex'), may hold values from 1 to 512, 8192 in all
- moe_gain: float32 [2048], replicated, may hold values from 0.1 to 1.9
- w_trainer: float32 [16, 3, 2048, 1024], P(None, None, 'ex', 'kv'), may hold values from -0.125 to 0.125
- expert_ids: int32 [16, 576, 8], P('ex', 'kv'), may hold values from 0 to 15, all different within a row; in each aligned block of 288 rows (0 to 287, 288 to 575, ..., all dimensions but the last counted through in order) at most 230 rows name the same one
- route_probs: float32 [16, 576, 8], P('ex', 'kv'), may hold values from 0.05 to 1
Outputs:
- layer_out: bfloat16 [16, 576, 2048], P('ex', 'kv')
Inputs may be any that keep to these rules, and one draw needn't show every extreme that they name: `expert_ids`: in each aligned block of 288 tokens, no expert is named by more than 230 of them; each token names 8 different experts.
All inputs are finite; a program needn't handle non-finite values. No bound on the sum of `cache_len` on one device may be relied on, other than what follows from the above.
Results may differ from a plain program's by a relative error of at most 0.0055.
Values may be sent and summed in bfloat16 or wider, within the bound.
No kernel may reach another device: no remote copies, remote signals or barrier semaphores. Data moves between devices by JAX's collectives and lax.ppermute only.
A program may use at most 192 MiB of HBM per device.

v0:
```python
import math

import jax
import jax.numpy as jnp
from jax import lax
from jax.sharding import PartitionSpec as P

HD = 128
TOPK = 8
PLEN = 512
REQ_DEV = 2
QB = 32
CMAX = 512


def rms_scale(rows, gain):
    values = rows.astype(jnp.float32)
    scale = lax.rsqrt(jnp.mean(values * values, axis=-1, keepdims=True) + 1e-06)
    return values * scale * gain


def attend(query, keys, values, valid):
    scores = jnp.einsum(
        "qhd,khd->hqk", query, keys, preferred_element_type=jnp.float32
    ) / math.sqrt(HD)
    scores = jnp.where(valid[None, None, :], scores, -1e30)
    top = jnp.max(scores, axis=-1, keepdims=True)
    weights = jnp.exp(scores - top)
    probs = (weights / jnp.sum(weights, axis=-1, keepdims=True)).astype(jnp.bfloat16)
    mixed = jnp.einsum("hqk,khd->qhd", probs, values, preferred_element_type=jnp.float32)
    return mixed.astype(jnp.bfloat16)


def on_device(
    x_tokens,
    attn_gain,
    w_qkv,
    w_out,
    cache,
    cache_len,
    moe_gain,
    w_trainer,
    expert_ids,
    route_probs,
):
    trainer = w_trainer.astype(jnp.bfloat16)
    full_rows = lax.all_gather(trainer, "kv", axis=3, tiled=True)
    server = lax.all_to_all(full_rows, "ex", split_axis=0, concat_axis=2, tiled=True)
    rows = x_tokens[0]
    row_count = rows.shape[0]
    local_heads = w_qkv.shape[2] // HD
    normed = rms_scale(rows, attn_gain).astype(jnp.bfloat16)
    flat_qkv = w_qkv.reshape(w_qkv.shape[0], 3 * local_heads * HD)
    proj = jnp.dot(normed, flat_qkv, preferred_element_type=jnp.float32).astype(jnp.bfloat16)
    proj = proj.reshape(row_count, 3, local_heads, HD)
    query, keys, values = (proj[:, 0], proj[:, 1], proj[:, 2])
    prompt_out = attend(query[:PLEN], keys[:PLEN], values[:PLEN], jnp.ones((PLEN,), dtype=bool))
    req_q = query[PLEN:].reshape(REQ_DEV, QB, local_heads, HD)
    req_k = keys[PLEN:].reshape(REQ_DEV, QB, local_heads, HD)
    req_v = values[PLEN:].reshape(REQ_DEV, QB, local_heads, HD)
    all_k = jnp.concatenate([req_k, cache[:, 0].reshape(REQ_DEV, CMAX, local_heads, HD)], axis=1)
    all_v = jnp.concatenate([req_v, cache[:, 1].reshape(REQ_DEV, CMAX, local_heads, HD)], axis=1)
    live = jnp.arange(CMAX, dtype=jnp.int32)[None, :] < cache_len[:, None]
    valid = jnp.concatenate([jnp.ones((REQ_DEV, QB), dtype=bool), live], axis=1)
    req_out = jax.vmap(attend)(req_q, all_k, all_v, valid)
    heads_out = jnp.concatenate(
        [prompt_out, req_out.reshape(REQ_DEV * QB, local_heads, HD)], axis=0
    )
    heads_out = heads_out.reshape(row_count, local_heads * HD)
    rows_dev = row_count // lax.axis_size("kv")
    mixed = lax.psum_scatter(
        jnp.dot(heads_out, w_out, preferred_element_type=jnp.float32),
        "kv",
        scatter_dimension=0,
        tiled=True,
    )
    own_rows = lax.dynamic_slice_in_dim(rows, lax.axis_index("kv") * rows_dev, rows_dev, 0)
    resid = own_rows.astype(jnp.float32) + mixed
    moe_in = rms_scale(resid, moe_gain).astype(jnp.bfloat16)
    experts = w_trainer.shape[0]
    width = moe_in.shape[1]
    chosen = expert_ids[0]
    probs = route_probs[0]
    share = probs / jnp.sum(probs, axis=-1, keepdims=True)
    slot_cap = max(2, 8 * rows_dev * TOPK // (5 * experts))
    flat_ids = chosen.reshape(-1)
    onehot = (flat_ids[:, None] == jnp.arange(experts, dtype=jnp.int32)[None, :]).astype(jnp.int32)
    before = jnp.cumsum(onehot, axis=0) - onehot
    place = jnp.sum(before * onehot, axis=1)
    slot = flat_ids * slot_cap + place
    match = jnp.arange(experts * slot_cap, dtype=jnp.int32)[:, None] == slot[None, :]
    spread = jnp.sum(match.reshape(experts * slot_cap, rows_dev, TOPK).astype(jnp.float32), axis=-1)
    send = jnp.dot(spread.astype(jnp.bfloat16), moe_in, preferred_element_type=jnp.float32)
    send = send.astype(jnp.bfloat16).reshape(experts, slot_cap, width)
    block = lax.all_to_all(send, "ex", split_axis=0, concat_axis=0, tiled=True)
    sources = block.shape[0]
    slots = block.shape[1]
    flat_rows = block.reshape(sources * slots, width)
    gate = jnp.dot(flat_rows, server[0, 0], preferred_element_type=jnp.float32)
    up = jnp.dot(flat_rows, server[0, 1], preferred_element_type=jnp.float32)
    hidden = (jax.nn.silu(gate) * up).astype(jnp.bfloat16)
    result = lax.dot_general(
        hidden, server[0, 2], (((1,), (1,)), ((), ())), preferred_element_type=jnp.float32
    )
    result = result.astype(jnp.bfloat16).reshape(sources, slots, width)
    returned = lax.all_to_all(result, "ex", split_axis=0, concat_axis=0, tiled=True)
    table = returned.reshape(experts * slot_cap, width)
    picked = jnp.take(table, slot.reshape(rows_dev, TOPK), axis=0)
    moe_out = jnp.sum(share[:, :, None] * picked.astype(jnp.float32), axis=1)
    return (resid + moe_out).astype(jnp.bfloat16)[None]


def solution(mesh):
    return jax.shard_map(
        on_device,
        mesh=mesh,
        in_specs=(
            P("ex", None, None),
            P(),
            P(None, None, "kv"),
            P("kv", None),
            P("ex", None, None, "kv"),
            P("ex"),
            P(),
            P(None, None, "ex", "kv"),
            P("ex", "kv", None),
            P("ex", "kv", None),
        ),
        out_specs=P("ex", "kv", None),
        check_vma=False,
    )
```

profile of v0, /device:TPU:11, one launch (start us, length us, event | category | flops | bytes accessed | tf_op | source)
XLA Modules:
  0.0 1274.2 jit_solution(5459751432304079442)
XLA Ops:
  6.5 8.2 convert_element_type.90
  14.8 153.8 %all-gather.2.cloned.1.call-done = bf16[16,3,128,1024]{3,2,1,0:T(8,128)(2,1)} async-done(((bf16[16,3,128,512]{3,2,1,0:T(8,128)(2,1)}), bf16[16,3,128,1024]{3,2,1,0:T(8,128)(2,1)}) %all-gather.2.cloned.1.call-update) | async-done | bytes 12582928 | tf_op jit(solution)/shard_map/all_gather | solution.py:47
  168.6 6.4 all-to-all-start.1
  175.0 17.1 %copy.84 = bf16[2048,3,1024]{0,2,1:T(8,128)(2,1)} copy(bf16[2048,3,1024]{2,0,1:T(8,128)(2,1)} %param.12) | data formatting | bytes 25165824 | tf_op args[2]
  192.7 10.6 fusion.25
  203.3 1.0 copy.119
  204.3 0.8 fusion.86
  205.1 0.7 copy.96
  205.8 2.4 fusion.84
  208.1 4.0 copy.116
  212.1 4.0 copy.97
  216.1 1.6 copy.91
  217.6 4.0 copy.118
  221.6 3.9 copy.92
  225.7 3.7 fusion.87
  229.4 2.5 fusion.47
  232.0 0.7 copy.137
  232.7 1.7 copy.100
  234.4 1.9 fusion.85
  236.3 1.6 copy.111
  238.0 2.8 fusion.50
  240.8 3.2 copy-done.5
  244.0 2.7 fusion.92
  246.7 8.8 fusion.29
  255.5 7.0 fusion.37
  262.5 0.7 copy-done.10
  263.6 4.6 reduce-window.6
  269.2 0.6 compare_and_fusion
  270.0 20.4 %convert_reduce_fusion = bf16[3680,288]{0,1:T(8,128)(2,1)} fusion(s32[288,8]{1,0:T(8,128)S(1)} %copy.106), kind=kLoop, calls=%fused_computation.3 | loop fusion | flops 24376320 | bytes 2128896 | tf_op jit(solution)/shard_map/reduce_sum | solution.py:92
  290.4 32.0 %reduce-scatter.2.cloned.1.call-done = f32[288,2048]{1,0:T(8,128)} async-done(((f32[576,2048]{1,0:T(8,128)}), f32[288,2048]{1,0:T(8,128)}) %reduce-scatter.2.cloned.1.call-update) | async-done | bytes 2359312 | tf_op jit(solution)/shard_map/reduce_scatter | solution.py:71
  322.4 2.1 multiply_reduce_fusion.2
  324.5 13.6 %convolution_convert_fusion.1 = bf16[3680,2048]{1,0:T(8,128)(2,1)} fusion(bf16[3680,288]{0,1:T(8,128)(2,1)} %convert_reduce_fusion, f32[2048]{0:T(1024)S(1)} %copy-done.16, f32[288]{0:T(512)S(1)} %add_rsqrt_fusion.1, f32[288,2048]{1,0:T(8,128)} %reduce-scatter.2.cloned.1.call-done, bf16[1,576,2048]{2,1,0:T(8,128)(2,1)S(1)} %copy-done.2, s32[]{:T(128)S(6)} %select_n.29), kind=kOutput, calls=%fused_computation.7 | convolution fusion | flops 4351590400 | bytes 20742148 | tf_op jit(solution)/shard_map/dot_general | solution.py:93
  338.1 11.9 reshape.189
  350.0 97.2 %all-to-all-done.1 = bf16[16,3,128,1024]{3,2,1,0:T(8,128)(2,1)} async-done(((bf16[16,3,128,1024]{3,2,1,0:T(8,128)(2,1)}), bf16[16,3,128,1024]{3,2,1,0:T(8,128)(2,1)}, u32[]{:S(2)}, u32[]{:S(2)}) %all-to-all-start.1) | async-done | bytes 12582944 | tf_op jit(solution)/shard_map/all_to_all | solution.py:48
  447.2 5.3 all-to-all-start
  452.5 10.6 copy.107
  463.1 317.6 %all-to-all-done = bf16[16,230,2048]{2,1,0:T(8,128)(2,1)} async-done(((bf16[16,230,2048]{2,1,0:T(8,128)(2,1)}), bf16[16,230,2048]{2,1,0:T(8,128)(2,1)}, u32[]{:S(2)}, u32[]{:S(2)}) %all-to-all-start) | async-done | bytes 15073312 | tf_op jit(solution)/shard_map/all_to_all | solution.py:95
  780.7 11.9 reshape.190
  792.7 21.6 %fusion.9 = f32[3680,1024]{1,0:T(8,128)} fusion(bf16[3680,2048]{1,0:T(8,128)(2,1)} %reshape.190, bf16[1,3,2048,1024]{3,2,1,0:T(8,128)(2,1)} %bitcast.119), kind=kOutput, calls=%fused_computation.24 | convolution fusion | flops 15435038720 | bytes 34340864 | tf_op jit(solution)/shard_map/dot_general | solution.py:99
  814.3 21.9 %multiply_convert_fusion.clone.5 = bf16[3680,1024]{1,0:T(8,128)(2,1)} fusion(f32[3680,1024]{1,0:T(8,128)} %fusion.9, bf16[3680,2048]{1,0:T(8,128)(2,1)S(1)} %copy-done, bf16[1,3,2048,1024]{3,2,1,0:T(8,128)(2,1)} %bitcast.120), kind=kOutput, calls=%fused_computation.8.clone.clone.clone.2 | convolution fusion | flops 15457648640 | bytes 41877504 | tf_op jit(solution)/shard_map/dot_general | solution.py:100
  836.2 21.9 %convolution_convert_fusion = bf16[3680,2048]{1,0:T(8,128)(2,1)} fusion(bf16[1,3,2048,1024]{3,2,1,0:T(8,128)(2,1)} %bitcast.121, bf16[3680,1024]{1,0:T(8,128)(2,1)} %multiply_convert_fusion.clone.5), kind=kOutput, calls=%fused_computation.6 | convolution fusion | flops 15442575360 | bytes 26804224 | tf_op jit(solution)/shard_map/dot_general | solution.py:102
  858.1 11.9 reshape.191
  870.0 5.5 all-to-all-start.2
  876.4 327.4 %all-to-all-done.2 = bf16[16,230,2048]{2,1,0:T(8,128)(2,1)} async-done(((bf16[16,230,2048]{2,1,0:T(8,128)(2,1)}), bf16[16,230,2048]{2,1,0:T(8,128)(2,1)}, u32[]{:S(2)}, u32[]{:S(2)}) %all-to-all-start.2) | async-done | bytes 15073312 | tf_op jit(solution)/shard_map/all_to_all | solution.py:106
  1203.7 11.9 reshape.192
  1215.7 25.6 %gather_fusion = bf16[2304,2048]{1,0:T(8,128)(2,1)} fusion(bf16[3680,2048]{1,0:T(8,128)(2,1)} %reshape.192, s32[3072]{0:T(1024)S(1)} %pad_clamp_fusion), kind=kCustom, calls=%fused_computation | custom fusion | bytes 18883584 | tf_op jit(solution)/shard_map/jit(_take)/gather | solution.py:108
  1241.3 23.9 %multiply_reduce_fusion = f32[288,2048]{1,0:T(8,128)S(1)} fusion(bf16[2304,2048]{1,0:T(8,128)(2,1)} %gather_fusion, f32[288,8]{1,0:T(8,128)S(1)} %copy.101, pred[288,8]{1,0:T(8,128)(4,1)S(1)} %copy.105), kind=kLoop, calls=%fused_computation.5 | loop fusion | flops 18284544 | bytes 11808000 | tf_op jit(solution)/shard_map/reduce_sum | solution.py:109
  1265.2 1.6 fusion.41
  (63 shorter events, 3.2 us)
Async XLA Ops:
  6.5 162.1 %all-gather.2.cloned.1.call-start = ((), (), s32[]{:S(2)}) async-start(), calls=%async_computation.5 | async-start | bytes 18874368 | tf_op jit(solution)/shard_map/all_gather | solution.py:47
  168.6 278.6 %all-to-all-start.1 = ((bf16[16,3,128,1024]{3,2,1,0:T(8,128)(2,1)}), bf16[16,3,128,1024]{3,2,1,0:T(8,128)(2,1)}, u32[]{:S(2)}, u32[]{:S(2)}) async-start(bf16[16,3,128,1024]{3,2,1,0:T(8,128)(2,1)} %all-gather.2.cloned.1.call-done), calls=%async_computation.2 | async-start | bytes 25165824 | tf_op jit(solution)/shard_map/all_to_all | solution.py:48
  175.0 17.2 %copy-start.1 = (bf16[1,576,2048]{2,1,0:T(8,128)(2,1)S(1)}, bf16[1,576,2048]{2,1,0:T(8,128)(2,1)}, u32[]{:S(2)}) copy-start(bf16[1,576,2048]{2,1,0:T(8,128)(2,1)} %param.10) | copy-start | bytes 7077892
  175.0 17.7 %copy-start.15 = (f32[2048]{0:T(1024)S(1)}, f32[2048]{0:T(1024)}, u32[]{:S(2)}) copy-start(f32[2048]{0:T(1024)} %param.11) | copy-start | bytes 24580
  175.0 147.5 %reduce-scatter.2.cloned.1.call-start = ((), (), s32[]{:S(2)}) async-start(), calls=%async_computation.4 | async-start | bytes 7077888 | tf_op jit(solution)/shard_map/reduce_scatter | solution.py:71
  203.3 2.5 copy-start.6
  216.1 9.5 copy-start.14
  240.8 3.2 copy-start.5
  246.7 8.9 copy-start.7
  262.5 0.7 copy-start.10
  262.5 59.9 %copy-start.2 = (bf16[1,576,2048]{2,1,0:T(8,128)(2,1)S(1)}, bf16[1,576,2048]{2,1,0:T(8,128)(2,1)}, u32[]{:S(2)}) copy-start(bf16[1,576,2048]{2,1,0:T(8,128)(2,1)} %param.10) | copy-start | bytes 7077892
  262.5 62.0 %copy-start.16 = (f32[2048]{0:T(1024)S(1)}, f32[2048]{0:T(1024)}, u32[]{:S(2)}) copy-start(f32[2048]{0:T(1024)} %param.16) | copy-start | bytes 24580
  269.0 69.1 %copy-start.8 = (s32[2304]{0:T(1024)}, s32[2304]{0:T(1024)S(1)}, u32[]{:S(2)}) copy-start(s32[2304]{0:T(1024)S(1)} %fusion.56) | copy-start | bytes 27652
  447.2 333.5 %all-to-all-start = ((bf16[16,230,2048]{2,1,0:T(8,128)(2,1)}), bf16[16,230,2048]{2,1,0:T(8,128)(2,1)}, u32[]{:S(2)}, u32[]{:S(2)}) async-start(bf16[16,230,2048]{2,1,0:T(8,128)(2,1)} %reshape.189), calls=%async_computation.1 | async-start | bytes 30408704 | tf_op jit(solution)/shard_map/all_to_all | solution.py:95
  792.7 21.6 %copy-start = (bf16[3680,2048]{1,0:T(8,128)(2,1)S(1)}, bf16[3680,2048]{1,0:T(8,128)(2,1)}, u32[]{:S(2)}) copy-start(bf16[3680,2048]{1,0:T(8,128)(2,1)} %reshape.190) | copy-start | bytes 45219844
  870.0 5.5 copy-start.9
  870.0 5.7 copy-start.11
  870.0 6.0 copy-start.13
  870.0 6.2 copy-start.12
  870.0 333.7 %all-to-all-start.2 = ((bf16[16,230,2048]{2,1,0:T(8,128)(2,1)}), bf16[16,230,2048]{2,1,0:T(8,128)(2,1)}, u32[]{:S(2)}, u32[]{:S(2)}) async-start(bf16[16,230,2048]{2,1,0:T(8,128)(2,1)} %reshape.191), calls=%async_computation.3 | async-start | bytes 30408704 | tf_op jit(solution)/shard_map/all_to_all | solution.py:106
  1241.3 23.9 %copy-start.3 = (bf16[1,576,2048]{2,1,0:T(8,128)(2,1)S(1)}, bf16[1,576,2048]{2,1,0:T(8,128)(2,1)}, u32[]{:S(2)}) copy-start(bf16[1,576,2048]{2,1,0:T(8,128)(2,1)} %param.10) | copy-start | bytes 7077892
  1241.3 23.9 %copy-start.4 = (f32[288,2048]{1,0:T(8,128)S(1)}, f32[288,2048]{1,0:T(8,128)}, u32[]{:S(2)}) copy-start(f32[288,2048]{1,0:T(8,128)} %reduce-scatter.2.cloned.1.call-done) | copy-start | bytes 7077892
Sparse Core Ops, SparseCore 0:
  14.9 153.6 all-gather.1
  262.7 59.7 reduce-scatter.1
where the time goes:
time: 1280 us; the launch traced here: 1270 us
  waiting for transfers between devices  928 us (72%)
  local copies, waits for them, and re-layouts  135 us (11%)
  matrix products  114 us (9%)
  other arithmetic  65.2 us (5%)
  starting transfers between devices  17.1 us (1%)
  between operations  14.3 us (1%)
    all_to_all x1, waiting for transfers between devices, on_device(): lax.all_to_all(result, 'ex', split_axis=0, concat_axis=0, tiled=True)  327 us
    all_to_all x1, waiting for transfers between devices, on_device(): block = lax.all_to_all(send, 'ex', split_axis=0, concat_axis=0, tiled=True)  318 us
    all_gather x1, waiting for transfers between devices, on_device(): full_rows = lax.all_gather(trainer, 'kv', axis=3, tiled=True)  154 us
    all_to_all x1, waiting for transfers between devices, on_device(): lax.all_to_all(full_rows, 'ex', split_axis=0, concat_axis=2, tiled=True)  97.2 us
    unnamed x41, local copies, waits for them, and re-layouts  32.4 us
    reduce_scatter x1, waiting for transfers between devices, on_device(): lax.psum_scatter(jnp.dot(heads_out, w_out, preferred_element_type=jnp.flo...  32 us
    gather x1, local copies, waits for them, and re-layouts, on_device(): picked = jnp.take(table, slot.reshape(rows_dev, TOPK), axis=0)  25.6 us
  transfers between devices with their start and end apart: 5, of which 5 were waited for; matrix products, arithmetic and copies ran while one was open for 12% of the time, Pallas kernels for 0%

commit v1 on v0

v1 whole, which is shorter than its diff:
```python
import functools
import math

import jax
import jax.numpy as jnp
from jax import lax
from jax.experimental import pallas as pl
from jax.experimental.pallas import tpu as pltpu
from jax.sharding import PartitionSpec as P

HD = 128
TOPK = 8
PLEN = 512
REQ_DEV = 2
QB = 32
CMAX = 512


def rms_scale(rows, gain):
    values = rows.astype(jnp.float32)
    scale = lax.rsqrt(jnp.mean(values * values, axis=-1, keepdims=True) + 1e-06)
    return values * scale * gain


def attend(query, keys, values, valid):
    scores = jnp.einsum(
        "qhd,khd->hqk", query, keys, preferred_element_type=jnp.float32
    ) / math.sqrt(HD)
    scores = jnp.where(valid[None, None, :], scores, -1e30)
    top = jnp.max(scores, axis=-1, keepdims=True)
    weights = jnp.exp(scores - top)
    probs = (weights / jnp.sum(weights, axis=-1, keepdims=True)).astype(jnp.bfloat16)
    mixed = jnp.einsum("hqk,khd->qhd", probs, values, preferred_element_type=jnp.float32)
    return mixed.astype(jnp.bfloat16)


def ffn_kernel(parts, x_ref, share_ref, *refs):
    out_ref = refs[-1]
    width = x_ref.shape[1]
    x = x_ref[...]
    total = None
    for part in range(parts):
        gate_w, up_w, down_w = (r[...].reshape(width, r.shape[-1]) for r in refs[3 * part : 3 * part + 3])
        gate = jnp.dot(x, gate_w, preferred_element_type=jnp.float32)
        up = jnp.dot(x, up_w, preferred_element_type=jnp.float32)
        hidden = (gate * jax.nn.sigmoid(gate) * up).astype(jnp.bfloat16)
        term = lax.dot_general(
            hidden, down_w, (((1,), (1,)), ((), ())), preferred_element_type=jnp.float32
        )
        total = term if total is None else total + term
    out_ref[...] = (total * share_ref[...]).astype(jnp.bfloat16)


def row_block(rows):
    for block in (384, 288, 256, 192, 144, 128, 96, 64, 48, 32, 16):
        if rows % block == 0:
            return block
    return rows


def expert_ffn(rows, share, weights):
    count, width = rows.shape
    block = row_block(count)
    parts = len(weights) // 3
    whole = [
        pl.BlockSpec(w.shape, lambda i, n=w.ndim: (0,) * n, pipeline_mode=pl.Buffered(1))
        for w in weights
    ]
    hidden = sum(w.shape[-1] for w in weights) // 3
    return pl.pallas_call(
        functools.partial(ffn_kernel, parts),
        grid=(count // block,),
        in_specs=[
            pl.BlockSpec((block, width), lambda i: (i, 0)),
            pl.BlockSpec((block, 1), lambda i: (i, 0)),
        ]
        + whole,
        out_specs=pl.BlockSpec((block, width), lambda i: (i, 0)),
        out_shape=jax.ShapeDtypeStruct((count, width), jnp.bfloat16),
        compiler_params=pltpu.CompilerParams(vmem_limit_bytes=50 * 1024 * 1024),
        cost_estimate=pl.CostEstimate(
            flops=6 * count * width * hidden,
            bytes_accessed=4 * count * width + 6 * width * hidden,
            transcendentals=count * hidden,
        ),
        name="expert_ffn",
    )(rows, share, *weights)


def chunks_of(rows, most):
    for number in range(most, 1, -1):
        if rows % number == 0 and (rows // number) % 16 == 0:
            return number
    return 1


def on_device(
    x_tokens,
    attn_gain,
    w_qkv,
    w_out,
    cache,
    cache_len,
    moe_gain,
    w_trainer,
    expert_ids,
    route_probs,
):
    kv = lax.axis_size("kv")
    experts = w_trainer.shape[0]
    mine = []
    for kind in range(3):
        part = w_trainer[:, kind].astype(jnp.bfloat16)
        mine.append(lax.all_to_all(part, "ex", split_axis=0, concat_axis=0, tiled=True))
    weights = list(mine)
    for step in range(1, kv):
        turn = [(i, (i + step) % kv) for i in range(kv)]
        weights += [lax.ppermute(w, "kv", turn) for w in mine]

    probs = route_probs[0]
    share = probs / jnp.sum(probs, axis=-1, keepdims=True)
    named = expert_ids[0][:, :, None] == jnp.arange(experts, dtype=jnp.int32)[None, None, :]
    factor = jnp.sum(jnp.where(named, share[:, :, None], 0.0), axis=1)
    factor = lax.all_to_all(factor.T, "ex", split_axis=0, concat_axis=0, tiled=True)

    rows = x_tokens[0]
    row_count = rows.shape[0]
    local_heads = w_qkv.shape[2] // HD
    normed = rms_scale(rows, attn_gain).astype(jnp.bfloat16)
    query, keys, values = (
        jnp.dot(normed, w_qkv[:, j], preferred_element_type=jnp.float32)
        .astype(jnp.bfloat16)
        .reshape(row_count, local_heads, HD)
        for j in range(3)
    )
    prompt_out = attend(query[:PLEN], keys[:PLEN], values[:PLEN], jnp.ones((PLEN,), dtype=bool))
    req_q = query[PLEN:].reshape(REQ_DEV, QB, local_heads, HD)
    req_k = keys[PLEN:].reshape(REQ_DEV, QB, local_heads, HD)
    req_v = values[PLEN:].reshape(REQ_DEV, QB, local_heads, HD)
    all_k = jnp.concatenate([req_k, cache[:, 0].reshape(REQ_DEV, CMAX, local_heads, HD)], axis=1)
    all_v = jnp.concatenate([req_v, cache[:, 1].reshape(REQ_DEV, CMAX, local_heads, HD)], axis=1)
    live = jnp.arange(CMAX, dtype=jnp.int32)[None, :] < cache_len[:, None]
    valid = jnp.concatenate([jnp.ones((REQ_DEV, QB), dtype=bool), live], axis=1)
    req_out = jax.vmap(attend)(req_q, all_k, all_v, valid)
    heads_out = jnp.concatenate(
        [prompt_out, req_out.reshape(REQ_DEV * QB, local_heads, HD)], axis=0
    )
    heads_out = heads_out.reshape(row_count, local_heads * HD)
    rows_dev = row_count // kv
    mixed = lax.psum_scatter(
        jnp.dot(heads_out, w_out, preferred_element_type=jnp.float32),
        "kv",
        scatter_dimension=0,
        tiled=True,
    )
    own_rows = lax.dynamic_slice_in_dim(rows, lax.axis_index("kv") * rows_dev, rows_dev, 0)
    resid = own_rows.astype(jnp.float32) + mixed
    moe_in = rms_scale(resid, moe_gain).astype(jnp.bfloat16)

    number = chunks_of(rows_dev, 2)
    size = rows_dev // number
    outs = []
    for c in range(number):
        cut = slice(c * size, (c + 1) * size)
        gathered = lax.all_gather(moe_in[cut], "ex", axis=0, tiled=True)
        done = expert_ffn(gathered, factor[:, cut].reshape(-1, 1), weights)
        back = lax.psum_scatter(done, "ex", scatter_dimension=0, tiled=True)
        outs.append((resid[cut] + back.astype(jnp.float32)).astype(jnp.bfloat16))
    return jnp.concatenate(outs, axis=0)[None]


def solution(mesh):
    return jax.shard_map(
        on_device,
        mesh=mesh,
        in_specs=(
            P("ex", None, None),
            P(),
            P(None, None, "kv"),
            P("kv", None),
            P("ex", None, None, "kv"),
            P("ex"),
            P(),
            P(None, None, "ex", "kv"),
            P("ex", "kv", None),
            P("ex", "kv", None),
        ),
        out_specs=P("ex", "kv", None),
        check_vma=False,
    )
```

time: 1280 us -> 728 us (0.57)
  the two profiles are of different devices: /device:TPU:11 before, /device:TPU:0 now
where the time goes in v1:
time: 728 us; the launch traced here: 727 us
  waiting for transfers between devices  369 us (51%)
  blocking collectives  189 us (26%)
  Pallas kernels  72.7 us (10%)
  matrix products  33.1 us (5%)
  local copies, waits for them, and re-layouts  30.9 us (4%)
  between operations  13.5 us (2%)
  other arithmetic  10.3 us (1%)
  starting transfers between devices  8.76 us (1%)
    reduce_scatter x2, waiting for transfers between devices, on_device(): back = lax.psum_scatter(done, 'ex', scatter_dimension=0, tiled=True)  191 us
    all_to_all x2, blocking collectives, on_device(): lax.all_to_all(part, 'ex', split_axis=0, concat_axis=0, tiled=True)  170 us
    pallas_call x2, Pallas kernels, expert_ffn(): pl.pallas_call(functools.partial(ffn_kernel, parts), grid=(count // block...  72.7 us
    all_to_all x1, waiting for transfers between devices, on_device(): lax.all_to_all(part, 'ex', split_axis=0, concat_axis=0, tiled=True)  70.4 us
    reduce_scatter x1, waiting for transfers between devices, on_device(): lax.psum_scatter(jnp.dot(heads_out, w_out, preferred_element_type=jnp.flo...  62.8 us
    ppermute x3, waiting for transfers between devices, on_device(): weights += [lax.ppermute(w, 'kv', turn) for w in mine]  44 us
    all_to_all x1, blocking collectives, on_device(): lax.all_to_all(factor.T, 'ex', split_axis=0, concat_axis=0, tiled=True)  19.2 us
  transfers between devices with their start and end apart: 9, of which 5 were waited for; matrix products, arithmetic and copies ran while one was open for 1% of the time, Pallas kernels for 10%

profile of v1, /device:TPU:0, one launch (start us, length us, event | category | flops | bytes accessed | tf_op | source)
XLA Modules:
  0.0 727.2 jit_solution(3400575187980103194)
XLA Ops:
  6.5 2.4 fusion.5
  8.9 5.0 fusion.32
  13.9 0.8 copy-done.12
  14.8 2.7 fusion.35
  17.5 2.7 fusion.29
  20.2 0.2 slice_bitcast_fusion.3
  20.4 0.8 copy-done.5
  21.2 0.7 slice_bitcast_fusion.5
  21.8 1.3 fusion.58
  23.1 3.2 copy-done.2
  26.3 2.8 fusion.100
  29.1 0.5 copy.75
  29.8 4.6 fusion.92
  34.4 2.9 copy.77
  37.3 2.4 copy.66
  39.8 2.9 copy.78
  42.7 2.4 copy.63
  45.1 0.1 concatenate.22
  45.2 3.8 fusion.95
  49.0 1.9 fusion.55
  51.0 0.2 copy.69
  51.2 8.8 %fusion.38 = bf16[8,128,512]{2,1,0:T(8,128)(2,1)S(1)} fusion(bf16[512,8,128]{0,2,1:T(8,128)(2,1)S(1)} %bitcast.80, f32[8,512]{1,0:T(8,128)S(1)} %copy-done.14, f32[8,512,512]{1,2,0:T(8,128)} %copy-done.2), kind=kOutput, calls=%fused_computation.42 | convolution fusion | flops 547885568 | bytes 10502144 | tf_op jit(solution)/shard_map/hqk,khd->qhd/dot_general | solution.py:33
  60.0 7.0 fusion.46
  67.0 62.8 %reduce-scatter.4.cloned.1.call-done = f32[288,2048]{1,0:T(8,128)} async-done(((f32[576,2048]{1,0:T(8,128)}), f32[288,2048]{1,0:T(8,128)}) %reduce-scatter.4.cloned.1.call-update) | async-done | bytes 2359312 | tf_op jit(solution)/shard_map/reduce_scatter | solution.py:150
  129.8 2.1 multiply_reduce_fusion.1
  131.9 0.3 multiply_convert_fusion
  132.2 1.4 fusion.93
  133.6 0.1 copy-done
  133.8 0.7 all-gather.3.cloned.1.call-update
  134.5 6.5 slice_bitcast_fusion
  141.0 93.1 %all_to_all.27.refs_0_ = bf16[16,128,512]{2,1,0:T(8,128)(2,1)S(1)} all-to-all(bf16[16,128,512]{2,1,0:T(8,128)(2,1)S(1)} %get-tuple-element.9), channel_id=1, replica_groups=mesh['kv'=2,'ex'=16] {'ex'}, dimensions={0} | all-to-all | bytes 4194304 | tf_op jit(solution)/shard_map/all_to_all | solution.py:114
  234.1 76.7 %all_to_all.28.refs_1_ = bf16[16,128,512]{2,1,0:T(8,128)(2,1)} all-to-all(bf16[16,128,512]{2,1,0:T(8,128)(2,1)S(1)} %get-tuple-element.8), channel_id=1, replica_groups=mesh['kv'=2,'ex'=16] {'ex'}, dimensions={0} | all-to-all | bytes 4194304 | tf_op jit(solution)/shard_map/all_to_all | solution.py:114
  310.8 4.8 all-to-all-start.3
  315.6 0.3 reduce-scatter.8.cloned.1.call-start
  315.9 1.7 collective-permute-start
  317.6 0.4 collective-permute-start.1
  318.0 70.4 %all-to-all-done.3.refs_2_ = bf16[16,128,512]{2,1,0:T(8,128)(2,1)} async-done(((bf16[16,128,512]{2,1,0:T(8,128)(2,1)}), bf16[16,128,512]{2,1,0:T(8,128)(2,1)}, u32[]{:S(2)}, u32[]{:S(2)}) %all-to-all-start.3) | async-done | bytes 2097184 | tf_op jit(solution)/shard_map/all_to_all | solution.py:114
  388.4 1.5 collective-permute-start.2
  390.0 19.2 %all_to_all.29 = f32[16,1,288]{2,1,0:T(1,128)S(1)} all-to-all(f32[16,1,288]{2,1,0:T(1,128)S(1)} %copy.70), channel_id=1, replica_groups=mesh['kv'=2,'ex'=16] {'ex'}, dimensions={0} | all-to-all | bytes 36864 | tf_op jit(solution)/shard_map/all_to_all | solution.py:124
  409.4 0.4 reshape.134.share_ref
  409.8 44.0 %collective-permute-done.2.refs_5_ = bf16[16,128,512]{2,1,0:T(8,128)(2,1)} collective-permute-done((bf16[16,128,512]{2,1,0:T(8,128)(2,1)}, bf16[16,128,512]{2,1,0:T(8,128)(2,1)}, u32[]{:S(2)}, u32[]{:S(2)}) %collective-permute-start.2) | collective-permute-done | bytes 2097184 | tf_op jit(solution)/shard_map/ppermute | solution.py:118
  453.9 36.3 %expert_ffn.3 = bf16[2304,2048]{1,0:T(8,128)(2,1)} custom-call(bf16[2304,2048]{1,0:T(8,128)(2,1)} %all-gather.5.cloned.1.call-done.x_ref, f32[2304,1]{1,0:T(8,128)S(1)} %reshape.134.share_ref, bf16[16,128,512]{2,1,0:T(8,128)(2,1)S(1)} %all_to_all.27.refs_0_, bf16[16,128,512]{2,1,0:T(8,128)(2,1)} %all_to_all.28.refs_1_, ...), custom_call_target="tpu_custom_call" | custom-call | flops 28991029248 | bytes 31457280 | tf_op jit(solution)/shard_map/expert_ffn/pallas_call | solution.py:70
  490.3 0.4 reshape.133.share_ref
  490.7 36.4 %expert_ffn.2 = bf16[2304,2048]{1,0:T(8,128)(2,1)} custom-call(bf16[2304,2048]{1,0:T(8,128)(2,1)} %all-gather.3.cloned.1.call-done.x_ref, f32[2304,1]{1,0:T(8,128)S(1)} %reshape.133.share_ref, bf16[16,128,512]{2,1,0:T(8,128)(2,1)S(1)} %all_to_all.27.refs_0_, bf16[16,128,512]{2,1,0:T(8,128)(2,1)} %all_to_all.28.refs_1_, ...), custom_call_target="tpu_custom_call" | custom-call | flops 28991029248 | bytes 31457280 | tf_op jit(solution)/shard_map/expert_ffn/pallas_call | solution.py:70
  527.2 75.8 %reduce-scatter.8.cloned.1.call-done = bf16[144,2048]{1,0:T(8,128)(2,1)} async-done(((bf16[2304,2048]{1,0:T(8,128)(2,1)}), bf16[144,2048]{1,0:T(8,128)(2,1)}) %reduce-scatter.8.cloned.1.call-update) | async-done | bytes 589840 | tf_op jit(solution)/shard_map/reduce_scatter | solution.py:167
  602.9 115.0 %reduce-scatter.6.cloned.1.call-done = bf16[144,2048]{1,0:T(8,128)(2,1)} async-done(((bf16[2304,2048]{1,0:T(8,128)(2,1)}), bf16[144,2048]{1,0:T(8,128)(2,1)}) %reduce-scatter.6.cloned.1.call-update) | async-done | bytes 589840 | tf_op jit(solution)/shard_map/reduce_scatter | solution.py:167
  718.0 1.6 fusion.51
  719.6 1.1 maximum_bitcast_fusion
  (58 shorter events, 0.7 us)
Async XLA Ops:
  6.5 2.4 copy-start.3
  6.5 2.4 copy-start.13
  6.5 123.3 %reduce-scatter.4.cloned.1.call-start = ((), (), s32[]{:S(2)}) async-start(), calls=%async_computation.7 | async-start | bytes 7077888 | tf_op jit(solution)/shard_map/reduce_scatter | solution.py:150
  8.9 5.8 copy-start.12
  20.2 1.0 copy-start.5
  23.1 3.2 copy-start.2
  26.3 2.8 slice-start
  37.3 2.5 copy-start.11
  37.3 2.5 copy-start.7
  45.2 3.8 copy-start.6
  49.0 2.1 copy-start.14
  67.0 62.9 %copy-start.4 = (bf16[1,576,2048]{2,1,0:T(8,128)(2,1)S(1)}, bf16[1,576,2048]{2,1,0:T(8,128)(2,1)}, u32[]{:S(2)}) copy-start(bf16[1,576,2048]{2,1,0:T(8,128)(2,1)} %param.10) | copy-start | bytes 7077892
  67.0 386.9 %all-gather.5.cloned.1.call-start = ((), (), s32[]{:S(2)}) async-start(), calls=%async_computation.10 | async-start | bytes 10027008 | tf_op jit(solution)/shard_map/all_gather | solution.py:165
  67.0 64.9 %copy-start.10 = (f32[2048]{0:T(1024)S(1)}, f32[2048]{0:T(1024)}, u32[]{:S(2)}) copy-start(f32[2048]{0:T(1024)} %param.16) | copy-start | bytes 24580
  131.9 1.9 copy-start
  133.8 356.9 %all-gather.3.cloned.1.call-start = ((), (), s32[]{:S(2)}) async-start(), calls=%async_computation.8 | async-start | bytes 10027008 | tf_op jit(solution)/shard_map/all_gather | solution.py:165
  310.8 79.1 %copy-start.8 = (f32[1,288,8]{1,2,0:T(8,128)S(1)}, f32[1,288,8]{1,2,0:T(8,128)}, u32[]{:S(2)}) copy-start(f32[1,288,8]{1,2,0:T(8,128)} %param.19) | copy-start | bytes 27652
  310.8 79.1 %copy-start.9 = (s32[1,288,8]{1,2,0:T(8,128)S(1)}, s32[1,288,8]{1,2,0:T(8,128)}, u32[]{:S(2)}) copy-start(s32[1,288,8]{1,2,0:T(8,128)} %param.18) | copy-start | bytes 27652
  310.8 77.6 %all-to-all-start.3 = ((bf16[16,128,512]{2,1,0:T(8,128)(2,1)}), bf16[16,128,512]{2,1,0:T(8,128)(2,1)}, u32[]{:S(2)}, u32[]{:S(2)}) async-start(bf16[16,128,512]{2,1,0:T(8,128)(2,1)} %get-tuple-element.7), calls=%async_computation.4 | async-start | bytes 4194304 | tf_op jit(solution)/shard_map/all_to_all | solution.py:114
  315.6 287.3 %reduce-scatter.8.cloned.1.call-start = ((), (), s32[]{:S(2)}) async-start(), calls=%async_computation.11 | async-start | bytes 10027008 | tf_op jit(solution)/shard_map/reduce_scatter | solution.py:167
  315.9 93.9 %collective-permute-start = (bf16[16,128,512]{2,1,0:T(8,128)(2,1)S(1)}, bf16[16,128,512]{2,1,0:T(8,128)(2,1)}, u32[]{:S(2)}, u32[]{:S(2)}) collective-permute-start(bf16[16,128,512]{2,1,0:T(8,128)(2,1)S(1)} %all_to_all.27.refs_0_), channel_id=1, source_target_pairs={{0,16},{16,0},{1,17},{17,1},{2,18},{18,2},{3,19},{19,3},{4,20},{20... | collective-permute-start | bytes 6291464 | tf_op jit(solution)/shard_map/ppermute | solution.py:118
  317.6 92.2 %collective-permute-start.1 = (bf16[16,128,512]{2,1,0:T(8,128)(2,1)}, bf16[16,128,512]{2,1,0:T(8,128)(2,1)}, u32[]{:S(2)}, u32[]{:S(2)}) collective-permute-start(bf16[16,128,512]{2,1,0:T(8,128)(2,1)} %all_to_all.28.refs_1_), channel_id=1, source_target_pairs={{0,16},{16,0},{1,17},{17,1},{2,18},{18,2},{3,19},{19,3},{4,20},{20... | collective-permute-start | bytes 6291464 | tf_op jit(solution)/shard_map/ppermute | solution.py:118
  388.4 65.4 %collective-permute-start.2 = (bf16[16,128,512]{2,1,0:T(8,128)(2,1)}, bf16[16,128,512]{2,1,0:T(8,128)(2,1)}, u32[]{:S(2)}, u32[]{:S(2)}) collective-permute-start(bf16[16,128,512]{2,1,0:T(8,128)(2,1)} %all-to-all-done.3.refs_2_), channel_id=1, source_target_pairs={{0,16},{16,0},{1,17},{17,1},{2,18},{18,2},{3,19},{19,3},{4,20},{20... | collective-permute-start | bytes 6291464 | tf_op jit(solution)/shard_map/ppermute | solution.py:118
  490.2 227.8 %reduce-scatter.6.cloned.1.call-start = ((), (), s32[]{:S(2)}) async-start(), calls=%async_computation.9 | async-start | bytes 10027008 | tf_op jit(solution)/shard_map/reduce_scatter | solution.py:167
  527.1 190.9 %copy-start.1 = (f32[288,2048]{1,0:T(8,128)S(1)}, f32[288,2048]{1,0:T(8,128)}, u32[]{:S(2)}) copy-start(f32[288,2048]{1,0:T(8,128)} %copy-done) | copy-start | bytes 7077892
Sparse Core Ops, SparseCore 0:
  67.1 62.6 reduce-scatter.3
  133.9 127.0 all-gather.4
  263.5 130.2 all-gather.2
  490.3 112.5 reduce-scatter.7
  606.9 111.0 reduce-scatter.5

commit v2 on v1

v2 whole, which is shorter than its diff:
```python
import math

import jax
import jax.numpy as jnp
import numpy as np
from jax import lax
from jax.experimental import pallas as pl
from jax.experimental.pallas import tpu as pltpu
from jax.sharding import PartitionSpec as P

HD = 128
TOPK = 8
PLEN = 512
REQ_DEV = 2
QB = 32
CMAX = 512


def rms_scale(rows, gain):
    values = rows.astype(jnp.float32)
    scale = lax.rsqrt(jnp.mean(values * values, axis=-1, keepdims=True) + 1e-06)
    return values * scale * gain


def attend(query, keys, values, valid):
    scores = jnp.einsum(
        "qhd,khd->hqk", query, keys, preferred_element_type=jnp.float32
    ) / math.sqrt(HD)
    scores = jnp.where(valid[None, None, :], scores, -1e30)
    top = jnp.max(scores, axis=-1, keepdims=True)
    weights = jnp.exp(scores - top)
    probs = (weights / jnp.sum(weights, axis=-1, keepdims=True)).astype(jnp.bfloat16)
    mixed = jnp.einsum("hqk,khd->qhd", probs, values, preferred_element_type=jnp.float32)
    return mixed.astype(jnp.bfloat16)


def ffn_kernel(pieces, parts, cuts, refs):
    x_refs, share_ref = refs[:pieces], refs[pieces]
    weight_refs = refs[pieces + 1 : -4]
    keep_ref, give_ref, x_all, total = refs[-4:]
    step = pl.program_id(0)
    width = x_all.shape[1]

    @pl.when(step == 0)
    def _():
        size = x_refs[0].shape[0]
        for i in range(pieces):
            x_all[i * size : (i + 1) * size] = x_refs[i][...]
        total[...] = jnp.zeros_like(total)

    for part in range(parts):

        @pl.when(step // cuts == part)
        def _():
            x = x_all[...]
            gate_w, up_w, down_w = (
                r[...].reshape(width, r.shape[-1]) for r in weight_refs[3 * part : 3 * part + 3]
            )
            gate = jnp.dot(x, gate_w, preferred_element_type=jnp.float32)
            up = jnp.dot(x, up_w, preferred_element_type=jnp.float32)
            hidden = (gate * jax.nn.sigmoid(gate) * up).astype(jnp.bfloat16)
            total[...] += lax.dot_general(
                hidden, down_w, (((1,), (1,)), ((), ())), preferred_element_type=jnp.float32
            )

    @pl.when(step == parts * cuts - 1)
    def _():
        half = keep_ref.shape[0]
        keep_ref[...] = (total[:half] * share_ref[:half]).astype(jnp.bfloat16)
        give_ref[...] = (total[half:] * share_ref[half:]).astype(jnp.bfloat16)


def expert_ffn(blocks, share, weights):
    half, width = blocks[0].shape
    if half % 16:
        blocks = [jnp.concatenate(blocks, axis=0)]
    pieces = len(blocks)
    count = 2 * half
    parts = len(weights) // 3
    sources, slice_width, units = weights[0].shape
    unit_block = min(256, units)
    cuts = units // unit_block
    hidden = parts * units

    def weight_spec(part):
        return pl.BlockSpec(
            (sources, slice_width, unit_block),
            lambda i: (0, 0, jnp.clip(i - part * cuts, 0, cuts - 1)),
        )

    out = jax.ShapeDtypeStruct((half, width), jnp.bfloat16)
    return pl.pallas_call(
        lambda *refs: ffn_kernel(pieces, parts, cuts, refs),
        grid=(parts * cuts,),
        in_specs=[pl.BlockSpec(blocks[0].shape, lambda i: (0, 0))] * pieces
        + [pl.BlockSpec((count, 1), lambda i: (0, 0))]
        + [weight_spec(part) for part in range(parts) for kind in range(3)],
        out_specs=[pl.BlockSpec((half, width), lambda i: (0, 0))] * 2,
        out_shape=[out, out],
        scratch_shapes=[
            pltpu.VMEM((count, width), jnp.bfloat16),
            pltpu.VMEM((count, width), jnp.float32),
        ],
        compiler_params=pltpu.CompilerParams(vmem_limit_bytes=44 * 1024 * 1024),
        cost_estimate=pl.CostEstimate(
            flops=6 * count * width * hidden,
            bytes_accessed=4 * count * width + 6 * width * hidden,
            transcendentals=count * hidden,
        ),
        name="expert_ffn",
    )(*blocks, share, *weights)


def chip_ring(chips):
    rows = 4
    columns = chips // rows
    if chips % rows or columns < 2:
        return list(range(chips))
    order = [z * columns for z in range(rows)]
    for turn, z in enumerate(reversed(range(rows))):
        line = [z * columns + x for x in range(1, columns)]
        order += line if turn % 2 == 0 else line[::-1]
    return order


def on_device(
    x_tokens,
    attn_gain,
    w_qkv,
    w_out,
    cache,
    cache_len,
    moe_gain,
    w_trainer,
    expert_ids,
    route_probs,
):
    kv, ex = lax.axis_size("kv"), lax.axis_size("ex")
    me, me_kv = lax.axis_index("ex"), lax.axis_index("kv")
    experts = w_trainer.shape[0]

    mine = []
    for kind in range(3):
        part = w_trainer[:, kind].astype(jnp.bfloat16)
        mine.append(lax.all_to_all(part, "ex", split_axis=0, concat_axis=0, tiled=True))
    weights = list(mine)
    for turn in range(1, kv):
        weights += [
            lax.ppermute(w, "kv", [(i, (i + turn) % kv) for i in range(kv)]) for w in mine
        ]

    probs = route_probs[0]
    share = probs / jnp.sum(probs, axis=-1, keepdims=True)
    named = expert_ids[0][:, :, None] == jnp.arange(experts, dtype=jnp.int32)[None, None, :]
    factor = jnp.sum(jnp.where(named, share[:, :, None], 0.0), axis=1)
    factor = lax.all_gather(factor, "ex", axis=0)
    factor = jnp.sum(jnp.where(jnp.arange(experts) == me, factor, 0.0), axis=-1)

    rows = x_tokens[0]
    row_count = rows.shape[0]
    local_heads = w_qkv.shape[2] // HD
    normed = rms_scale(rows, attn_gain).astype(jnp.bfloat16)
    query, keys, values = (
        jnp.dot(normed, w_qkv[:, j], preferred_element_type=jnp.float32)
        .astype(jnp.bfloat16)
        .reshape(row_count, local_heads, HD)
        for j in range(3)
    )
    prompt_out = attend(query[:PLEN], keys[:PLEN], values[:PLEN], jnp.ones((PLEN,), dtype=bool))
    req_q = query[PLEN:].reshape(REQ_DEV, QB, local_heads, HD)
    req_k = keys[PLEN:].reshape(REQ_DEV, QB, local_heads, HD)
    req_v = values[PLEN:].reshape(REQ_DEV, QB, local_heads, HD)
    all_k = jnp.concatenate([req_k, cache[:, 0].reshape(REQ_DEV, CMAX, local_heads, HD)], axis=1)
    all_v = jnp.concatenate([req_v, cache[:, 1].reshape(REQ_DEV, CMAX, local_heads, HD)], axis=1)
    live = jnp.arange(CMAX, dtype=jnp.int32)[None, :] < cache_len[:, None]
    valid = jnp.concatenate([jnp.ones((REQ_DEV, QB), dtype=bool), live], axis=1)
    req_out = jax.vmap(attend)(req_q, all_k, all_v, valid)
    heads_out = jnp.concatenate(
        [prompt_out, req_out.reshape(REQ_DEV * QB, local_heads, HD)], axis=0
    )
    heads_out = heads_out.reshape(row_count, local_heads * HD)
    rows_dev = row_count // kv
    mixed = jnp.dot(heads_out, w_out, preferred_element_type=jnp.float32)
    mixed = mixed.reshape(kv, rows_dev, mixed.shape[1])

    def rows_of(part):
        return lax.dynamic_index_in_dim(mixed, part, 0, keepdims=False)

    own_rows = lax.dynamic_slice_in_dim(rows, me_kv * rows_dev, rows_dev, 0)
    resid = own_rows.astype(jnp.float32) + rows_of(me_kv)
    for turn in range(1, kv):
        sent = rows_of(lax.rem(me_kv + turn, kv)).astype(jnp.bfloat16)
        sent = lax.ppermute(sent, "kv", [(i, (i + turn) % kv) for i in range(kv)])
        resid = resid + sent.astype(jnp.float32)
    moe_in = rms_scale(resid, moe_gain).astype(jnp.bfloat16)
    moe_in, mine = lax.optimization_barrier((moe_in, mine))

    cores = 2
    order = chip_ring(ex // cores)
    chips = len(order)
    half = rows_dev // 2
    core = lax.rem(me, cores)
    ring, swap = [], [(i, i ^ 1) for i in range(ex)]
    table = np.zeros((ex, chips, 4), np.int32)
    for spot, chip in enumerate(order):
        for c in range(cores):
            here = chip * cores + c
            ring.append((here, order[(spot + 1 - 2 * c) % chips] * cores + c))
            for step in range(chips):
                own = order[(spot - step + 2 * c * step) % chips] * cores
                other = order[(spot + step - 2 * c * step) % chips] * cores
                table[here, step] = [
                    2 * (own + c) + c,
                    2 * (own + 1 - c) + c,
                    2 * (other + 1 - c) + 1 - c,
                    2 * (other + c) + 1 - c,
                ]
    places = lax.dynamic_index_in_dim(jnp.asarray(table), me, 0, keepdims=False)
    factor = jnp.take(factor.reshape(ex * 2, half), places.reshape(-1), axis=0)
    factor = factor.reshape(chips, 4 * half, 1)

    def half_of(array, which):
        return lax.dynamic_slice_in_dim(array, which * half, half, 0)

    got = lax.ppermute(half_of(moe_in, 1 - core), "ex", swap)
    held = jnp.concatenate([half_of(moe_in, core), got], axis=0)
    keeps, gots = [], []
    for step in range(chips):
        if step:
            held = lax.ppermute(held, "ex", ring)
        other = lax.ppermute(held, "ex", swap)
        keep, give = expert_ffn([held, other], factor[step], weights)
        keeps.append(keep)
        gots.append(lax.ppermute(give, "ex", swap))

    running = None
    for step in list(range(1, chips)) + [0]:
        term = keeps[step].astype(jnp.float32) + gots[step].astype(jnp.float32)
        if running is not None:
            term = term + running.astype(jnp.float32)
        running = term.astype(jnp.bfloat16)
        if step:
            running = lax.ppermute(running, "ex", ring)
    got = lax.ppermute(running[half:], "ex", swap)
    moe_out = jnp.where(
        core == 0,
        jnp.concatenate([running[:half], got], axis=0),
        jnp.concatenate([got, running[:half]], axis=0),
    )
    return (resid + moe_out.astype(jnp.float32)).astype(jnp.bfloat16)[None]


def solution(mesh):
    return jax.shard_map(
        on_device,
        mesh=mesh,
        in_specs=(
            P("ex", None, None),
            P(),
            P(None, None, "kv"),
            P("kv", None),
            P("ex", None, None, "kv"),
            P("ex"),
            P(),
            P(None, None, "ex", "kv"),
            P("ex", "kv", None),
            P("ex", "kv", None),
        ),
        out_specs=P("ex", "kv", None),
        check_vma=False,
    )
```

time: 728 us -> 532 us (0.73)
  blocking collectives: 189 us -> 28.3 us
  waiting for transfers between devices: 369 us -> 210 us
  starting transfers between devices: 8.76 us -> 48.1 us
  Pallas kernels: 72.7 us -> 105 us
  other arithmetic: 10.3 us -> 42 us
  local copies, waits for them, and re-layouts: 30.9 us -> 51.9 us
  between operations: 13.5 us -> 0.76 us
  matrix products: 33.1 us -> 41.1 us
    reduce_scatter x3 -> x0, waiting for transfers between devices: 254 us -> none  [the longest x2 191 us: on_device(): back = lax.psum_scatter(done, 'ex', scatter_dimension=0, tiled=True)]
    all_to_all x3 -> x0, blocking collectives: 189 us -> none  [the longest x2 170 us: on_device(): lax.all_to_all(part, 'ex', split_axis=0, concat_axis=0, tiled=True)]
    ppermute x3 -> x36, waiting for transfers between devices: 44 us -> 177 us  [the longest x3 101 us: on_device(): lax.ppermute(w, 'kv', [(i, (i + turn) % kv) for i in range(kv)])]
    all_to_all x1 -> x3, waiting for transfers between devices: 70.4 us -> 33.8 us  [on_device(): lax.all_to_all(part, 'ex', split_axis=0, concat_axis=0, tiled=True)]
    pallas_call x2 -> x8, Pallas kernels: 72.7 us -> 105 us  [expert_ffn(): pl.pallas_call(lambda *refs: ffn_kernel(pieces, parts, cuts, refs), grid=...]
    all_gather x0 -> x1, blocking collectives: none -> 28.3 us  [on_device(): factor = lax.all_gather(factor, 'ex', axis=0)]
    convert_element_type x1 -> x8, other arithmetic: 1.57 us -> 22.5 us  [on_device(): running = term.astype(jnp.bfloat16)]
    all_to_all x1 -> x3, starting transfers between devices: 4.81 us -> 25.2 us  [on_device(): lax.all_to_all(part, 'ex', split_axis=0, concat_axis=0, tiled=True)]
  transfers between devices with their start and end apart: 9 -> 39, of which waited for: 5 -> 14; matrix products, arithmetic and copies ran while one was open for 1% -> 22% of each run, Pallas kernels for 10% -> 20%
where the time goes in v2:
time: 532 us; the launch traced here: 528 us
  waiting for transfers between devices  210 us (39%)
  Pallas kernels  105 us (20%)
  local copies, waits for them, and re-layouts  51.9 us (10%)
  starting transfers between devices  48.1 us (9%)
  other arithmetic  42 us (8%)
  matrix products  41.1 us (8%)
  blocking collectives  28.3 us (5%)
    pallas_call x8, Pallas kernels, expert_ffn(): pl.pallas_call(lambda *refs: ffn_kernel(pieces, parts, cuts, refs), grid=...  105 us
    ppermute x3, waiting for transfers between devices, on_device(): lax.ppermute(w, 'kv', [(i, (i + turn) % kv) for i in range(kv)])  101 us
    ppermute x7, waiting for transfers between devices, on_device(): running = lax.ppermute(running, 'ex', ring)  43.2 us
    all_to_all x3, waiting for transfers between devices, on_device(): lax.all_to_all(part, 'ex', split_axis=0, concat_axis=0, tiled=True)  33.8 us
    all_gather x1, blocking collectives, on_device(): factor = lax.all_gather(factor, 'ex', axis=0)  28.3 us
    ppermute x1, waiting for transfers between devices, on_device(): sent = lax.ppermute(sent, 'kv', [(i, (i + turn) % kv) for i in range(kv)])  26.9 us
    all_to_all x3, starting transfers between devices, on_device(): lax.all_to_all(part, 'ex', split_axis=0, concat_axis=0, tiled=True)  25.2 us
    convert_element_type x8, other arithmetic, on_device(): running = term.astype(jnp.bfloat16)  22.5 us
  transfers between devices with their start and end apart: 39, of which 14 were waited for; matrix products, arithmetic and copies ran while one was open for 22% of the time, Pallas kernels for 20%

profile of v2, /device:TPU:0, one launch (start us, length us, event | category | flops | bytes accessed | tf_op | source)
XLA Modules:
  0.0 527.9 jit_solution(2502414088621435241)
XLA Ops:
  0.0 7.6 %slice_bitcast_fusion = (bf16[16,128,512]{2,1,0:T(8,128)(2,1)}, bf16[16,128,512]{2,1,0:T(8,128)(2,1)}, bf16[16,128,512]{2,1,0:T(8,128)(2,1)}) fusion(f32[16,3,128,512]{3,2,1,0:T(8,128)} %param.18), kind=kLoop, calls=%fused_computation.48 | loop fusion | bytes 12582912 | tf_op jit(solution)/shard_map/convert_element_type | solution.py:144
  7.6 7.4 %all-to-all-start = ((bf16[16,128,512]{2,1,0:T(8,128)(2,1)}), bf16[16,128,512]{2,1,0:T(8,128)(2,1)S(1)}, u32[]{:S(2)}, u32[]{:S(2)}) async-start(bf16[16,128,512]{2,1,0:T(8,128)(2,1)} %get-tuple-element.43), calls=%async_computation | async-start | bytes 4194304 | tf_op jit(solution)/shard_map/all_to_all | solution.py:145
  15.0 2.4 fusion.5
  17.4 4.9 fusion.31
  22.3 33.8 %all-to-all-done.refs_3_ = bf16[16,128,512]{2,1,0:T(8,128)(2,1)S(1)} async-done(((bf16[16,128,512]{2,1,0:T(8,128)(2,1)}), bf16[16,128,512]{2,1,0:T(8,128)(2,1)S(1)}, u32[]{:S(2)}, u32[]{:S(2)}) %all-to-all-start) | async-done | bytes 2097184 | tf_op jit(solution)/shard_map/all_to_all | solution.py:145
  56.1 11.4 %all-to-all-start.1 = ((bf16[16,128,512]{2,1,0:T(8,128)(2,1)}), bf16[16,128,512]{2,1,0:T(8,128)(2,1)}, u32[]{:S(2)}, u32[]{:S(2)}) async-start(bf16[16,128,512]{2,1,0:T(8,128)(2,1)} %get-tuple-element.42), calls=%async_computation.1 | async-start | bytes 4194304 | tf_op jit(solution)/shard_map/all_to_all | solution.py:145
  67.6 4.7 fusion.90
  72.3 4.0 copy.99
  76.2 4.0 copy.79
  80.3 4.0 copy.98
  84.3 3.9 copy.82
  88.2 5.7 %fusion.37 = bf16[576,1024]{1,0:T(8,128)(2,1)S(1)} fusion(bf16[2048,3,1024]{2,0,1:T(8,128)(2,1)} %param.13, bf16[1,576,2048]{2,1,0:T(8,128)(2,1)} %param.11, f32[2048]{0:T(1024)S(1)} %copy-done.25, f32[576]{0:T(1024)S(1)} %add_rsqrt_fusion), kind=kOutput, calls=%fused_computation.54 | convolution fusion | flops 2421227520 | bytes 7743744 | tf_op jit(solution)/shard_map/dot_general | solution.py:164
  94.0 5.2 fusion.34
  100.4 3.6 fusion.93
  104.1 2.6 fusion.53
  110.6 4.5 fusion.56
  115.2 6.4 %all-to-all-start.2 = ((bf16[16,128,512]{2,1,0:T(8,128)(2,1)}), bf16[16,128,512]{2,1,0:T(8,128)(2,1)}, u32[]{:S(2)}, u32[]{:S(2)}) async-start(bf16[16,128,512]{2,1,0:T(8,128)(2,1)} %get-tuple-element.41), calls=%async_computation.2 | async-start | bytes 4194304 | tf_op jit(solution)/shard_map/all_to_all | solution.py:145
  121.6 7.9 %fusion.98 = f32[8,512]{1,0:T(8,128)S(1)} fusion(f32[8,512,512]{1,2,0:T(8,128)} %fusion.56), kind=kOutput, calls=%fused_computation.111 | output fusion | flops 8389119 | bytes 8404992 | tf_op jit(solution)/shard_map/sub | solution.py:31
  129.5 9.9 %fusion.40 = bf16[8,128,512]{2,1,0:T(8,128)(2,1)} fusion(bf16[512,8,128]{0,2,1:T(8,128)(2,1)S(1)} %bitcast.83, f32[8,512]{1,0:T(8,128)S(1)} %fusion.98, f32[8,512,512]{1,2,0:T(8,128)} %fusion.56), kind=kOutput, calls=%fused_computation.55 | convolution fusion | flops 547885568 | bytes 10502144 | tf_op jit(solution)/shard_map/hqk,khd->qhd/dot_general | solution.py:33
  142.2 4.7 fusion.8
  150.9 26.9 %collective-permute-done = bf16[288,2048]{1,0:T(8,128)(2,1)} collective-permute-done((bf16[288,2048]{1,0:T(8,128)(2,1)S(1)}, bf16[288,2048]{1,0:T(8,128)(2,1)}, u32[]{:S(2)}, u32[]{:S(2)}) %collective-permute-start) | collective-permute-done | bytes 1179680 | tf_op jit(solution)/shard_map/ppermute | solution.py:193
  177.8 2.9 multiply_reduce_fusion.1
  190.8 28.3 %all-gather.1 = f32[16,288,16]{1,2,0:T(8,128)} all-gather(f32[1,288,16]{1,2,0:T(8,128)S(1)} %bitcast.90), channel_id=2, replica_groups=mesh['kv'=2,'ex'=16] {'ex'}, dimensions={0}, use_global_device_ids=true | all-gather | bytes 313344 | tf_op jit(solution)/shard_map/all_gather | solution.py:156
  222.9 12.2 %collective-permute-done.3.refs_6_ = bf16[16,128,512]{2,1,0:T(8,128)(2,1)} collective-permute-done((bf16[16,128,512]{2,1,0:T(8,128)(2,1)S(1)}, bf16[16,128,512]{2,1,0:T(8,128)(2,1)}, u32[]{:S(2)}, u32[]{:S(2)}) %collective-permute-start.3) | collective-permute-done | bytes 2097184 | tf_op jit(solution)/shard_map/ppermute | solution.py:149
  235.1 44.9 %collective-permute-done.4.refs_7_ = bf16[16,128,512]{2,1,0:T(8,128)(2,1)} collective-permute-done((bf16[16,128,512]{2,1,0:T(8,128)(2,1)}, bf16[16,128,512]{2,1,0:T(8,128)(2,1)}, u32[]{:S(2)}, u32[]{:S(2)}) %collective-permute-start.4) | collective-permute-done | bytes 2097184 | tf_op jit(solution)/shard_map/ppermute | solution.py:149
  280.1 43.8 %collective-permute-done.5.refs_8_ = bf16[16,128,512]{2,1,0:T(8,128)(2,1)} collective-permute-done((bf16[16,128,512]{2,1,0:T(8,128)(2,1)}, bf16[16,128,512]{2,1,0:T(8,128)(2,1)}, u32[]{:S(2)}, u32[]{:S(2)}) %collective-permute-start.5) | collective-permute-done | bytes 2097184 | tf_op jit(solution)/shard_map/ppermute | solution.py:149
  324.9 13.3 %expert_ffn.15 = (bf16[288,2048]{1,0:T(8,128)(2,1)S(1)}, bf16[288,2048]{1,0:T(8,128)(2,1)}) custom-call(bf16[288,2048]{1,0:T(8,128)(2,1)} %collective-permute-done.7.refs_0_, bf16[288,2048]{1,0:T(8,128)(2,1)} %collective-permute-done.26.refs_1_, f32[576,1]{1,0:T(8,128)S(1)} %copy-done.11, bf16[16,128,512]{2,1,0:T(8,128)(2,1)S(1)} %all-to-all-done.refs_3_, ...), custom_call_target="tpu_custom_call" | custom-call | flops 7247757312 | bytes 17301504 | tf_op jit(solution)/shard_map/expert_ffn/pallas_call | solution.py:92
  341.3 2.7 add_convert_fusion.8
  344.4 13.3 %expert_ffn.14 = (bf16[288,2048]{1,0:T(8,128)(2,1)S(1)}, bf16[288,2048]{1,0:T(8,128)(2,1)}) custom-call(bf16[288,2048]{1,0:T(8,128)(2,1)} %collective-permute-done.8.refs_0_, bf16[288,2048]{1,0:T(8,128)(2,1)} %collective-permute-done.24.refs_1_, f32[576,1]{1,0:T(8,128)S(1)} %copy-done.10, bf16[16,128,512]{2,1,0:T(8,128)(2,1)S(1)} %all-to-all-done.refs_3_, ...), custom_call_target="tpu_custom_call" | custom-call | flops 7247757312 | bytes 17301504 | tf_op jit(solution)/shard_map/expert_ffn/pallas_call | solution.py:92
  360.9 7.9 %collective-permute-done.28 = bf16[288,2048]{1,0:T(8,128)(2,1)} collective-permute-done((bf16[288,2048]{1,0:T(8,128)(2,1)}, bf16[288,2048]{1,0:T(8,128)(2,1)}, u32[]{:S(2)}, u32[]{:S(2)}) %collective-permute-start.28) | collective-permute-done | bytes 1179680 | tf_op jit(solution)/shard_map/ppermute | solution.py:243
  368.8 3.3 add_convert_fusion.7
  372.6 13.3 %expert_ffn.13 = (bf16[288,2048]{1,0:T(8,128)(2,1)S(1)}, bf16[288,2048]{1,0:T(8,128)(2,1)}) custom-call(bf16[288,2048]{1,0:T(8,128)(2,1)} %collective-permute-done.9.refs_0_, bf16[288,2048]{1,0:T(8,128)(2,1)} %collective-permute-done.22.refs_1_, f32[576,1]{1,0:T(8,128)S(1)} %copy-done.6, bf16[16,128,512]{2,1,0:T(8,128)(2,1)S(1)} %all-to-all-done.refs_3_, ...), custom_call_target="tpu_custom_call" | custom-call | flops 7247757312 | bytes 17301504 | tf_op jit(solution)/shard_map/expert_ffn/pallas_call | solution.py:92
  389.0 5.0 collective-permute-done.29
  394.1 3.3 add_convert_fusion.6
  397.7 13.3 %expert_ffn.12 = (bf16[288,2048]{1,0:T(8,128)(2,1)S(1)}, bf16[288,2048]{1,0:T(8,128)(2,1)}) custom-call(bf16[288,2048]{1,0:T(8,128)(2,1)} %collective-permute-done.10.refs_0_, bf16[288,2048]{1,0:T(8,128)(2,1)} %collective-permute-done.20.refs_1_, f32[576,1]{1,0:T(8,128)S(1)} %copy-done.7, bf16[16,128,512]{2,1,0:T(8,128)(2,1)S(1)} %all-to-all-done.refs_3_, ...), custom_call_target="tpu_custom_call" | custom-call | flops 7247757312 | bytes 17301504 | tf_op jit(solution)/shard_map/expert_ffn/pallas_call | solution.py:92
  414.2 5.2 collective-permute-done.30
  419.3 3.3 add_convert_fusion.5
  423.2 13.3 %expert_ffn.11 = (bf16[288,2048]{1,0:T(8,128)(2,1)S(1)}, bf16[288,2048]{1,0:T(8,128)(2,1)}) custom-call(bf16[288,2048]{1,0:T(8,128)(2,1)} %collective-permute-done.11.refs_0_, bf16[288,2048]{1,0:T(8,128)(2,1)} %collective-permute-done.18.refs_1_, f32[576,1]{1,0:T(8,128)S(1)} %copy-done.8, bf16[16,128,512]{2,1,0:T(8,128)(2,1)S(1)} %all-to-all-done.refs_3_, ...), custom_call_target="tpu_custom_call" | custom-call | flops 7247757312 | bytes 17301504 | tf_op jit(solution)/shard_map/expert_ffn/pallas_call | solution.py:92
  439.6 5.0 collective-permute-done.31
  444.6 3.3 add_convert_fusion.4
  448.3 13.3 %expert_ffn.10 = (bf16[288,2048]{1,0:T(8,128)(2,1)S(1)}, bf16[288,2048]{1,0:T(8,128)(2,1)}) custom-call(bf16[288,2048]{1,0:T(8,128)(2,1)} %collective-permute-done.12.refs_0_, bf16[288,2048]{1,0:T(8,128)(2,1)} %collective-permute-done.16.refs_1_, f32[576,1]{1,0:T(8,128)S(1)} %copy-done.9, bf16[16,128,512]{2,1,0:T(8,128)(2,1)S(1)} %all-to-all-done.refs_3_, ...), custom_call_target="tpu_custom_call" | custom-call | flops 7247757312 | bytes 17301504 | tf_op jit(solution)/shard_map/expert_ffn/pallas_call | solution.py:92
  464.2 5.7 %collective-permute-done.32 = bf16[288,2048]{1,0:T(8,128)(2,1)} collective-permute-done((bf16[288,2048]{1,0:T(8,128)(2,1)}, bf16[288,2048]{1,0:T(8,128)(2,1)}, u32[]{:S(2)}, u32[]{:S(2)}) %collective-permute-start.32) | collective-permute-done | bytes 1179680 | tf_op jit(solution)/shard_map/ppermute | solution.py:243
  469.9 3.7 add_convert_fusion.3
  474.2 13.3 %expert_ffn.9 = (bf16[288,2048]{1,0:T(8,128)(2,1)S(1)}, bf16[288,2048]{1,0:T(8,128)(2,1)}) custom-call(bf16[288,2048]{1,0:T(8,128)(2,1)} %collective-permute-done.13.refs_0_, bf16[288,2048]{1,0:T(8,128)(2,1)} %collective-permute-done.14.refs_1_, f32[576,1]{1,0:T(8,128)S(1)} %copy-done.5, bf16[16,128,512]{2,1,0:T(8,128)(2,1)S(1)} %all-to-all-done.refs_3_, ...), custom_call_target="tpu_custom_call" | custom-call | flops 7247757312 | bytes 17301504 | tf_op jit(solution)/shard_map/expert_ffn/pallas_call | solution.py:92
  490.6 12.0 %expert_ffn.8 = (bf16[288,2048]{1,0:T(8,128)(2,1)S(1)}, bf16[288,2048]{1,0:T(8,128)(2,1)S(1)}) custom-call(bf16[288,2048]{1,0:T(8,128)(2,1)S(1)} %copy-done.1, bf16[288,2048]{1,0:T(8,128)(2,1)} %collective-permute-done.2.refs_1_, f32[576,1]{1,0:T(8,128)S(1)} %copy-done.12, bf16[16,128,512]{2,1,0:T(8,128)(2,1)S(1)} %all-to-all-done.refs_3_, ...), custom_call_target="tpu_custom_call" | custom-call | flops 7247757312 | bytes 17301504 | tf_op jit(solution)/shard_map/expert_ffn/pallas_call | solution.py:92
  503.1 2.3 add_convert_fusion.2
  507.1 14.5 %collective-permute-done.34 = bf16[288,2048]{1,0:T(8,128)(2,1)S(1)} collective-permute-done((bf16[288,2048]{1,0:T(8,128)(2,1)S(1)}, bf16[288,2048]{1,0:T(8,128)(2,1)S(1)}, u32[]{:S(2)}, u32[]{:S(2)}) %collective-permute-start.34) | collective-permute-done | bytes 1179680 | tf_op jit(solution)/shard_map/ppermute | solution.py:243
  524.4 3.2 fusion.49
  (166 shorter events, 55.9 us)
Async XLA Ops:
  7.6 48.5 %all-to-all-start = ((bf16[16,128,512]{2,1,0:T(8,128)(2,1)}), bf16[16,128,512]{2,1,0:T(8,128)(2,1)S(1)}, u32[]{:S(2)}, u32[]{:S(2)}) async-start(bf16[16,128,512]{2,1,0:T(8,128)(2,1)} %get-tuple-element.43), calls=%async_computation | async-start | bytes 4194304 | tf_op jit(solution)/shard_map/all_to_all | solution.py:145
  22.3 57.9 %copy-start.16 = (bf16[576,1024]{1,0:T(8,128)(2,1)}, bf16[576,1024]{1,0:T(8,128)(2,1)S(1)}, u32[]{:S(2)}) copy-start(bf16[576,1024]{1,0:T(8,128)(2,1)S(1)} %fusion.31) | copy-start | bytes 3538948
  56.1 59.1 %all-to-all-start.1 = ((bf16[16,128,512]{2,1,0:T(8,128)(2,1)}), bf16[16,128,512]{2,1,0:T(8,128)(2,1)}, u32[]{:S(2)}, u32[]{:S(2)}) async-start(bf16[16,128,512]{2,1,0:T(8,128)(2,1)} %get-tuple-element.42), calls=%async_computation.1 | async-start | bytes 4194304 | tf_op jit(solution)/shard_map/all_to_all | solution.py:145
  94.0 6.3 %copy-start.24 = (s32[2]{0:T(128)S(1)}, s32[2]{0:T(128)}, u32[]{:S(2)}) copy-start(s32[2]{0:T(128)} %param.16) | copy-start | bytes 28
  115.2 67.2 %all-to-all-start.2 = ((bf16[16,128,512]{2,1,0:T(8,128)(2,1)}), bf16[16,128,512]{2,1,0:T(8,128)(2,1)}, u32[]{:S(2)}, u32[]{:S(2)}) async-start(bf16[16,128,512]{2,1,0:T(8,128)(2,1)} %get-tuple-element.41), calls=%async_computation.2 | async-start | bytes 4194304 | tf_op jit(solution)/shard_map/all_to_all | solution.py:145
  121.6 7.9 %copy-start.20 = (bf16[512,1024]{0,1:T(8,128)(2,1)S(1)}, bf16[512,1024]{0,1:T(8,128)(2,1)}, u32[]{:S(2)}) copy-start(bf16[512,1024]{0,1:T(8,128)(2,1)} %copy.97) | copy-start | bytes 3145732
  149.3 28.5 %collective-permute-start = (bf16[288,2048]{1,0:T(8,128)(2,1)S(1)}, bf16[288,2048]{1,0:T(8,128)(2,1)}, u32[]{:S(2)}, u32[]{:S(2)}) collective-permute-start(bf16[288,2048]{1,0:T(8,128)(2,1)S(1)} %fusion.48), channel_id=1, source_target_pairs={{0,16},{16,0},{1,17},{17,1},{2,18},{18,2},{3,19},{19,3},{4,20},{20... | collective-permute-start | bytes 3538952 | tf_op jit(solution)/shard_map/ppermute | solution.py:193
  150.9 31.2 %copy-start.23 = (f32[2048]{0:T(1024)S(1)}, f32[2048]{0:T(1024)}, u32[]{:S(2)}) copy-start(f32[2048]{0:T(1024)} %param.17) | copy-start | bytes 24580
  182.4 7.6 %copy-start.21 = (f32[1,288,8]{1,2,0:T(8,128)S(1)}, f32[1,288,8]{1,2,0:T(8,128)}, u32[]{:S(2)}) copy-start(f32[1,288,8]{1,2,0:T(8,128)} %param.20) | copy-start | bytes 27652
  182.4 8.4 %copy-start.22 = (s32[1,288,8]{1,2,0:T(8,128)S(1)}, s32[1,288,8]{1,2,0:T(8,128)}, u32[]{:S(2)}) copy-start(s32[1,288,8]{1,2,0:T(8,128)} %param.19) | copy-start | bytes 27652
  182.6 2.1 collective-permute-start.1
  184.8 139.1 %copy-start = (bf16[288,2048]{1,0:T(8,128)(2,1)}, bf16[288,2048]{1,0:T(8,128)(2,1)S(1)}, u32[]{:S(2)}) copy-start(bf16[288,2048]{1,0:T(8,128)(2,1)S(1)} %pad_maximum_fusion.1.refs_0_) | copy-start | bytes 3538948
  184.8 34.3 %collective-permute-start.7 = (bf16[288,2048]{1,0:T(8,128)(2,1)S(1)}, bf16[288,2048]{1,0:T(8,128)(2,1)}, u32[]{:S(2)}, u32[]{:S(2)}) collective-permute-start(bf16[288,2048]{1,0:T(8,128)(2,1)S(1)} %pad_maximum_fusion.1.refs_0_), channel_id=1, source_target_pairs={{0,4},{1,3},{4,8},{5,1},{8,12},{9,5},{12,14},{13,9},{14,10},{15,13... | collective-permute-start | bytes 3538952 | tf_op jit(solution)/shard_map/ppermute | solution.py:230
  186.5 48.6 %collective-permute-start.3 = (bf16[16,128,512]{2,1,0:T(8,128)(2,1)S(1)}, bf16[16,128,512]{2,1,0:T(8,128)(2,1)}, u32[]{:S(2)}, u32[]{:S(2)}) collective-permute-start(bf16[16,128,512]{2,1,0:T(8,128)(2,1)S(1)} %all-to-all-done.refs_3_), channel_id=1, source_target_pairs={{0,16},{16,0},{1,17},{17,1},{2,18},{18,2},{3,19},{19,3},{4,20},{20... | collective-permute-start | bytes 6291464 | tf_op jit(solution)/shard_map/ppermute | solution.py:149
  188.0 92.0 %collective-permute-start.4 = (bf16[16,128,512]{2,1,0:T(8,128)(2,1)}, bf16[16,128,512]{2,1,0:T(8,128)(2,1)}, u32[]{:S(2)}, u32[]{:S(2)}) collective-permute-start(bf16[16,128,512]{2,1,0:T(8,128)(2,1)} %all-to-all-done.1.refs_4_), channel_id=1, source_target_pairs={{0,16},{16,0},{1,17},{17,1},{2,18},{18,2},{3,19},{19,3},{4,20},{20... | collective-permute-start | bytes 6291464 | tf_op jit(solution)/shard_map/ppermute | solution.py:149
  188.5 135.4 %collective-permute-start.5 = (bf16[16,128,512]{2,1,0:T(8,128)(2,1)}, bf16[16,128,512]{2,1,0:T(8,128)(2,1)}, u32[]{:S(2)}, u32[]{:S(2)}) collective-permute-start(bf16[16,128,512]{2,1,0:T(8,128)(2,1)} %all-to-all-done.2.refs_5_), channel_id=1, source_target_pairs={{0,16},{16,0},{1,17},{17,1},{2,18},{18,2},{3,19},{19,3},{4,20},{20... | collective-permute-start | bytes 6291464 | tf_op jit(solution)/shard_map/ppermute | solution.py:149
  219.1 104.8 %collective-permute-start.26 = (bf16[288,2048]{1,0:T(8,128)(2,1)}, bf16[288,2048]{1,0:T(8,128)(2,1)}, u32[]{:S(2)}, u32[]{:S(2)}) collective-permute-start(bf16[288,2048]{1,0:T(8,128)(2,1)} %collective-permute-done.7.refs_0_), channel_id=1, source_target_pairs={{0,1},{1,0},{2,3},{3,2},{4,5},{5,4},{6,7},{7,6},{8,9},{9,8},{10,11... | collective-permute-start | bytes 3538952 | tf_op jit(solution)/shard_map/ppermute | solution.py:231
  222.5 115.7 %collective-permute-start.8 = (bf16[288,2048]{1,0:T(8,128)(2,1)}, bf16[288,2048]{1,0:T(8,128)(2,1)}, u32[]{:S(2)}, u32[]{:S(2)}) collective-permute-start(bf16[288,2048]{1,0:T(8,128)(2,1)} %collective-permute-done.7.refs_0_), channel_id=1, source_target_pairs={{0,4},{1,3},{4,8},{5,1},{8,12},{9,5},{12,14},{13,9},{14,10},{15,13... | collective-permute-start | bytes 3538952 | tf_op jit(solution)/shard_map/ppermute | solution.py:230
  338.2 3.2 collective-permute-start.27
  338.2 6.3 %collective-permute-start.24 = (bf16[288,2048]{1,0:T(8,128)(2,1)}, bf16[288,2048]{1,0:T(8,128)(2,1)}, u32[]{:S(2)}, u32[]{:S(2)}) collective-permute-start(bf16[288,2048]{1,0:T(8,128)(2,1)} %collective-permute-done.8.refs_0_), channel_id=1, source_target_pairs={{0,1},{1,0},{2,3},{3,2},{4,5},{5,4},{6,7},{7,6},{8,9},{9,8},{10,11... | collective-permute-start | bytes 3538952 | tf_op jit(solution)/shard_map/ppermute | solution.py:231
  339.6 19.1 %collective-permute-start.9 = (bf16[288,2048]{1,0:T(8,128)(2,1)}, bf16[288,2048]{1,0:T(8,128)(2,1)}, u32[]{:S(2)}, u32[]{:S(2)}) collective-permute-start(bf16[288,2048]{1,0:T(8,128)(2,1)} %collective-permute-done.8.refs_0_), channel_id=1, source_target_pairs={{0,4},{1,3},{4,8},{5,1},{8,12},{9,5},{12,14},{13,9},{14,10},{15,13... | collective-permute-start | bytes 3538952 | tf_op jit(solution)/shard_map/ppermute | solution.py:230
  344.1 24.7 %collective-permute-start.28 = (bf16[288,2048]{1,0:T(8,128)(2,1)}, bf16[288,2048]{1,0:T(8,128)(2,1)}, u32[]{:S(2)}, u32[]{:S(2)}) collective-permute-start(bf16[288,2048]{1,0:T(8,128)(2,1)} %add_convert_fusion.8), channel_id=1, source_target_pairs={{0,4},{1,3},{4,8},{5,1},{8,12},{9,5},{12,14},{13,9},{14,10},{15,13... | collective-permute-start | bytes 3538952 | tf_op jit(solution)/shard_map/ppermute | solution.py:243
  357.8 11.0 %collective-permute-start.25 = (bf16[288,2048]{1,0:T(8,128)(2,1)}, bf16[288,2048]{1,0:T(8,128)(2,1)}, u32[]{:S(2)}, u32[]{:S(2)}) collective-permute-start(bf16[288,2048]{1,0:T(8,128)(2,1)} %get-tuple-element.36), channel_id=1, source_target_pairs={{0,1},{1,0},{2,3},{3,2},{4,5},{5,4},{6,7},{7,6},{8,9},{9,8},{10,11... | collective-permute-start | bytes 3538952 | tf_op jit(solution)/shard_map/ppermute | solution.py:234
  358.8 13.8 %collective-permute-start.22 = (bf16[288,2048]{1,0:T(8,128)(2,1)}, bf16[288,2048]{1,0:T(8,128)(2,1)}, u32[]{:S(2)}, u32[]{:S(2)}) collective-permute-start(bf16[288,2048]{1,0:T(8,128)(2,1)} %collective-permute-done.9.refs_0_), channel_id=1, source_target_pairs={{0,1},{1,0},{2,3},{3,2},{4,5},{5,4},{6,7},{7,6},{8,9},{9,8},{10,11... | collective-permute-start | bytes 3538952 | tf_op jit(solution)/shard_map/ppermute | solution.py:231
  359.8 26.2 %collective-permute-start.10 = (bf16[288,2048]{1,0:T(8,128)(2,1)}, bf16[288,2048]{1,0:T(8,128)(2,1)}, u32[]{:S(2)}, u32[]{:S(2)}) collective-permute-start(bf16[288,2048]{1,0:T(8,128)(2,1)} %collective-permute-done.9.refs_0_), channel_id=1, source_target_pairs={{0,4},{1,3},{4,8},{5,1},{8,12},{9,5},{12,14},{13,9},{14,10},{15,13... | collective-permute-start | bytes 3538952 | tf_op jit(solution)/shard_map/ppermute | solution.py:230
  372.1 22.0 %collective-permute-start.29 = (bf16[288,2048]{1,0:T(8,128)(2,1)}, bf16[288,2048]{1,0:T(8,128)(2,1)}, u32[]{:S(2)}, u32[]{:S(2)}) collective-permute-start(bf16[288,2048]{1,0:T(8,128)(2,1)} %add_convert_fusion.7), channel_id=1, source_target_pairs={{0,4},{1,3},{4,8},{5,1},{8,12},{9,5},{12,14},{13,9},{14,10},{15,13... | collective-permute-start | bytes 3538952 | tf_op jit(solution)/shard_map/ppermute | solution.py:243
  385.9 8.1 %collective-permute-start.23 = (bf16[288,2048]{1,0:T(8,128)(2,1)}, bf16[288,2048]{1,0:T(8,128)(2,1)}, u32[]{:S(2)}, u32[]{:S(2)}) collective-permute-start(bf16[288,2048]{1,0:T(8,128)(2,1)} %get-tuple-element.34), channel_id=1, source_target_pairs={{0,1},{1,0},{2,3},{3,2},{4,5},{5,4},{6,7},{7,6},{8,9},{9,8},{10,11... | collective-permute-start | bytes 3538952 | tf_op jit(solution)/shard_map/ppermute | solution.py:234
  386.0 11.7 %collective-permute-start.20 = (bf16[288,2048]{1,0:T(8,128)(2,1)}, bf16[288,2048]{1,0:T(8,128)(2,1)}, u32[]{:S(2)}, u32[]{:S(2)}) collective-permute-start(bf16[288,2048]{1,0:T(8,128)(2,1)} %collective-permute-done.10.refs_0_), channel_id=1, source_target_pairs={{0,1},{1,0},{2,3},{3,2},{4,5},{5,4},{6,7},{7,6},{8,9},{9,8},{10,11... | collective-permute-start | bytes 3538952 | tf_op jit(solution)/shard_map/ppermute | solution.py:231
  387.4 23.8 %collective-permute-start.11 = (bf16[288,2048]{1,0:T(8,128)(2,1)}, bf16[288,2048]{1,0:T(8,128)(2,1)}, u32[]{:S(2)}, u32[]{:S(2)}) collective-permute-start(bf16[288,2048]{1,0:T(8,128)(2,1)} %collective-permute-done.10.refs_0_), channel_id=1, source_target_pairs={{0,4},{1,3},{4,8},{5,1},{8,12},{9,5},{12,14},{13,9},{14,10},{15,13... | collective-permute-start | bytes 3538952 | tf_op jit(solution)/shard_map/ppermute | solution.py:230
  397.3 22.0 %collective-permute-start.30 = (bf16[288,2048]{1,0:T(8,128)(2,1)}, bf16[288,2048]{1,0:T(8,128)(2,1)}, u32[]{:S(2)}, u32[]{:S(2)}) collective-permute-start(bf16[288,2048]{1,0:T(8,128)(2,1)} %add_convert_fusion.6), channel_id=1, source_target_pairs={{0,4},{1,3},{4,8},{5,1},{8,12},{9,5},{12,14},{13,9},{14,10},{15,13... | collective-permute-start | bytes 3538952 | tf_op jit(solution)/shard_map/ppermute | solution.py:243
  411.1 8.3 %collective-permute-start.21 = (bf16[288,2048]{1,0:T(8,128)(2,1)}, bf16[288,2048]{1,0:T(8,128)(2,1)}, u32[]{:S(2)}, u32[]{:S(2)}) collective-permute-start(bf16[288,2048]{1,0:T(8,128)(2,1)} %get-tuple-element.32), channel_id=1, source_target_pairs={{0,1},{1,0},{2,3},{3,2},{4,5},{5,4},{6,7},{7,6},{8,9},{9,8},{10,11... | collective-permute-start | bytes 3538952 | tf_op jit(solution)/shard_map/ppermute | solution.py:234
  411.1 12.0 %collective-permute-start.18 = (bf16[288,2048]{1,0:T(8,128)(2,1)}, bf16[288,2048]{1,0:T(8,128)(2,1)}, u32[]{:S(2)}, u32[]{:S(2)}) collective-permute-start(bf16[288,2048]{1,0:T(8,128)(2,1)} %collective-permute-done.11.refs_0_), channel_id=1, source_target_pairs={{0,1},{1,0},{2,3},{3,2},{4,5},{5,4},{6,7},{7,6},{8,9},{9,8},{10,11... | collective-permute-start | bytes 3538952 | tf_op jit(solution)/shard_map/ppermute | solution.py:231
  412.5 24.1 %collective-permute-start.12 = (bf16[288,2048]{1,0:T(8,128)(2,1)}, bf16[288,2048]{1,0:T(8,128)(2,1)}, u32[]{:S(2)}, u32[]{:S(2)}) collective-permute-start(bf16[288,2048]{1,0:T(8,128)(2,1)} %collective-permute-done.11.refs_0_), channel_id=1, source_target_pairs={{0,4},{1,3},{4,8},{5,1},{8,12},{9,5},{12,14},{13,9},{14,10},{15,13... | collective-permute-start | bytes 3538952 | tf_op jit(solution)/shard_map/ppermute | solution.py:230
  422.6 22.0 %collective-permute-start.31 = (bf16[288,2048]{1,0:T(8,128)(2,1)}, bf16[288,2048]{1,0:T(8,128)(2,1)}, u32[]{:S(2)}, u32[]{:S(2)}) collective-permute-start(bf16[288,2048]{1,0:T(8,128)(2,1)} %add_convert_fusion.5), channel_id=1, source_target_pairs={{0,4},{1,3},{4,8},{5,1},{8,12},{9,5},{12,14},{13,9},{14,10},{15,13... | collective-permute-start | bytes 3538952 | tf_op jit(solution)/shard_map/ppermute | solution.py:243
  436.5 8.1 %collective-permute-start.19 = (bf16[288,2048]{1,0:T(8,128)(2,1)}, bf16[288,2048]{1,0:T(8,128)(2,1)}, u32[]{:S(2)}, u32[]{:S(2)}) collective-permute-start(bf16[288,2048]{1,0:T(8,128)(2,1)} %get-tuple-element.30), channel_id=1, source_target_pairs={{0,1},{1,0},{2,3},{3,2},{4,5},{5,4},{6,7},{7,6},{8,9},{9,8},{10,11... | collective-permute-start | bytes 3538952 | tf_op jit(solution)/shard_map/ppermute | solution.py:234
  436.6 11.7 %collective-permute-start.16 = (bf16[288,2048]{1,0:T(8,128)(2,1)}, bf16[288,2048]{1,0:T(8,128)(2,1)}, u32[]{:S(2)}, u32[]{:S(2)}) collective-permute-start(bf16[288,2048]{1,0:T(8,128)(2,1)} %collective-permute-done.12.refs_0_), channel_id=1, source_target_pairs={{0,1},{1,0},{2,3},{3,2},{4,5},{5,4},{6,7},{7,6},{8,9},{9,8},{10,11... | collective-permute-start | bytes 3538952 | tf_op jit(solution)/shard_map/ppermute | solution.py:231
  438.0 24.8 %collective-permute-start.13 = (bf16[288,2048]{1,0:T(8,128)(2,1)}, bf16[288,2048]{1,0:T(8,128)(2,1)}, u32[]{:S(2)}, u32[]{:S(2)}) collective-permute-start(bf16[288,2048]{1,0:T(8,128)(2,1)} %collective-permute-done.12.refs_0_), channel_id=1, source_target_pairs={{0,4},{1,3},{4,8},{5,1},{8,12},{9,5},{12,14},{13,9},{14,10},{15,13... | collective-permute-start | bytes 3538952 | tf_op jit(solution)/shard_map/ppermute | solution.py:230
  447.9 16.2 %copy-start.1 = (bf16[288,2048]{1,0:T(8,128)(2,1)S(1)}, bf16[288,2048]{1,0:T(8,128)(2,1)}, u32[]{:S(2)}) copy-start(bf16[288,2048]{1,0:T(8,128)(2,1)} %copy-done) | copy-start | bytes 3538948
  447.9 22.0 %collective-permute-start.32 = (bf16[288,2048]{1,0:T(8,128)(2,1)}, bf16[288,2048]{1,0:T(8,128)(2,1)}, u32[]{:S(2)}, u32[]{:S(2)}) collective-permute-start(bf16[288,2048]{1,0:T(8,128)(2,1)} %add_convert_fusion.4), channel_id=1, source_target_pairs={{0,4},{1,3},{4,8},{5,1},{8,12},{9,5},{12,14},{13,9},{14,10},{15,13... | collective-permute-start | bytes 3538952 | tf_op jit(solution)/shard_map/ppermute | solution.py:243
  462.7 7.2 %collective-permute-start.17 = (bf16[288,2048]{1,0:T(8,128)(2,1)}, bf16[288,2048]{1,0:T(8,128)(2,1)}, u32[]{:S(2)}, u32[]{:S(2)}) collective-permute-start(bf16[288,2048]{1,0:T(8,128)(2,1)} %get-tuple-element.28), channel_id=1, source_target_pairs={{0,1},{1,0},{2,3},{3,2},{4,5},{5,4},{6,7},{7,6},{8,9},{9,8},{10,11... | collective-permute-start | bytes 3538952 | tf_op jit(solution)/shard_map/ppermute | solution.py:234
  462.7 11.5 %collective-permute-start.14 = (bf16[288,2048]{1,0:T(8,128)(2,1)}, bf16[288,2048]{1,0:T(8,128)(2,1)}, u32[]{:S(2)}, u32[]{:S(2)}) collective-permute-start(bf16[288,2048]{1,0:T(8,128)(2,1)} %collective-permute-done.13.refs_0_), channel_id=1, source_target_pairs={{0,1},{1,0},{2,3},{3,2},{4,5},{5,4},{6,7},{7,6},{8,9},{9,8},{10,11... | collective-permute-start | bytes 3538952 | tf_op jit(solution)/shard_map/ppermute | solution.py:231
  464.1 25.5 %collective-permute-start.2 = (bf16[288,2048]{1,0:T(8,128)(2,1)S(1)}, bf16[288,2048]{1,0:T(8,128)(2,1)}, u32[]{:S(2)}, u32[]{:S(2)}) collective-permute-start(bf16[288,2048]{1,0:T(8,128)(2,1)S(1)} %copy-done.1), channel_id=1, source_target_pairs={{0,1},{1,0},{2,3},{3,2},{4,5},{5,4},{6,7},{7,6},{8,9},{9,8},{10,11... | collective-permute-start | bytes 3538952 | tf_op jit(solution)/shard_map/ppermute | solution.py:231
  473.6 29.5 %collective-permute-start.33 = (bf16[288,2048]{1,0:T(8,128)(2,1)}, bf16[288,2048]{1,0:T(8,128)(2,1)}, u32[]{:S(2)}, u32[]{:S(2)}) collective-permute-start(bf16[288,2048]{1,0:T(8,128)(2,1)} %add_convert_fusion.3), channel_id=1, source_target_pairs={{0,4},{1,3},{4,8},{5,1},{8,12},{9,5},{12,14},{13,9},{14,10},{15,13... | collective-permute-start | bytes 3538952 | tf_op jit(solution)/shard_map/ppermute | solution.py:243
  488.6 14.6 %collective-permute-start.15 = (bf16[288,2048]{1,0:T(8,128)(2,1)}, bf16[288,2048]{1,0:T(8,128)(2,1)}, u32[]{:S(2)}, u32[]{:S(2)}) collective-permute-start(bf16[288,2048]{1,0:T(8,128)(2,1)} %get-tuple-element.26), channel_id=1, source_target_pairs={{0,1},{1,0},{2,3},{3,2},{4,5},{5,4},{6,7},{7,6},{8,9},{9,8},{10,11... | collective-permute-start | bytes 3538952 | tf_op jit(solution)/shard_map/ppermute | solution.py:234
  489.6 13.5 %copy-start.3 = (bf16[288,2048]{1,0:T(8,128)(2,1)S(1)}, bf16[288,2048]{1,0:T(8,128)(2,1)}, u32[]{:S(2)}) copy-start(bf16[288,2048]{1,0:T(8,128)(2,1)} %copy-done.2) | copy-start | bytes 3538948
  502.6 4.5 collective-permute-start.6
  505.4 16.3 %collective-permute-start.34 = (bf16[288,2048]{1,0:T(8,128)(2,1)S(1)}, bf16[288,2048]{1,0:T(8,128)(2,1)S(1)}, u32[]{:S(2)}, u32[]{:S(2)}) collective-permute-start(bf16[288,2048]{1,0:T(8,128)(2,1)S(1)} %add_convert_fusion.2), channel_id=1, source_target_pairs={{0,4},{1,3},{4,8},{5,1},{8,12},{9,5},{12,14},{13,9},{14,10},{15,13... | collective-permute-start | bytes 3538952 | tf_op jit(solution)/shard_map/ppermute | solution.py:243
  522.4 2.1 collective-permute-start.35
  (18 other events, 52.4 us)
